TPU v7x, 32 devices: a whole 2x2x4 slice. The times are simulated.
32 devices in a mesh: tx: 8 (over z, core), ty: 2 (over y), mode: 2 (over x).
Axes of the slice: x: 2, y: 2, z: 4, core: 2. Of those that a mesh axis runs over, the one named last changes fastest.
Arguments:
- obj: float32 [2, 2048, 2048], P(None, 'tx', 'ty'), may hold values from -4 to 4
- probe: float32 [4, 2, 256, 256], P('mode'), may hold values from -4 to 4
- intensity: float32 [8, 2, 2, 256, 256], P('tx', 'ty'), may hold values from 0 to 2
- offsets: int32 [8, 2, 2, 2], P('tx', 'ty'), may hold values from 0 to 1023, as said below
- counts: int32 [8, 2], P('tx', 'ty'), may hold values from 1 to 2, as said below
- patch_filters: float32 [16, 4], replicated, may hold values from -2 to 2
Outputs:
- new_obj: float32 [2, 2048, 2048], P(None, 'tx', 'ty')
Inputs may be any that keep to these rules, and one draw needn't show every extreme that they name: Row offsets are below 256, column offsets below 1024; a pattern may reach into the tiles below and to the right. Slots from counts[a,b] on are empty.
All inputs are finite; a program needn't handle non-finite values.
Results may differ from a plain program's by a relative error of at most 0.00012.
Values sent between devices are 32-bit elements; how exact they have to be, the bound alone decides.
A program may use at most 128 MiB of HBM per device.

v0:
```python
import functools
import math

import jax
import jax.numpy as jnp
import ml_dtypes
import numpy as np
from jax import lax
from jax.experimental import pallas as pl
from jax.experimental.pallas import tpu as pltpu
from jax.sharding import PartitionSpec as P

highest = lax.Precision.HIGHEST
step_size = 0.25


def shift(value, steps_tx, steps_ty, tx, ty):
    if steps_tx and steps_ty:
        pairs = []
        for a in range(tx):
            for b in range(ty):
                to_a, to_b = a + steps_tx, b + steps_ty
                if 0 <= to_a < tx and 0 <= to_b < ty:
                    pairs.append((a * ty + b, to_a * ty + to_b))
        return lax.ppermute(value, ("tx", "ty"), pairs)
    axis, count, steps = ("tx", tx, steps_tx) if steps_tx else ("ty", ty, steps_ty)
    pairs = [(i, i + steps) for i in range(count) if 0 <= i + steps < count]
    return lax.ppermute(value, axis, pairs)


def split(value):
    top = value.astype(np.float32).astype(ml_dtypes.bfloat16)
    rest = (value - top.astype(np.float64)).astype(ml_dtypes.bfloat16)
    return top, rest


def tables(length):
    ramp = np.arange(length)
    angle = (ramp[:, None] * ramp[None, :] % length) * (2.0 * math.pi / length)
    c = np.cos(angle) / math.sqrt(length)
    s = -np.sin(angle) / math.sqrt(length)
    plain = np.block([[c, s], [-s, c]])
    conj = np.block([[c, -s], [s, c]])
    out = []
    for table in (plain, conj):
        top, rest = split(table)
        out.append(np.concatenate([top, top, rest], axis=0))
        out.append(np.concatenate([top, top, rest], axis=1))
    return out


def halves(value):
    top = value.astype(jnp.bfloat16)
    rest = (value - top.astype(jnp.float32)).astype(jnp.bfloat16)
    return top, rest


def dot_right(value, table):
    top, rest = halves(value)
    return jnp.dot(jnp.concatenate([top, rest, top], axis=1), table, preferred_element_type=jnp.float32)


def dot_left(table, value):
    top, rest = halves(value)
    return jnp.dot(table, jnp.concatenate([top, rest, top], axis=0), preferred_element_type=jnp.float32)


def slot_kernel(place_ref, patch_ref, probe_ref, measured_ref, pr_ref, pl_ref, cr_ref, cl_ref, grad_ref, wave_ref, rolled_ref, power_ref):
    modes, width = probe_ref.shape[0], probe_ref.shape[-1]
    row, col, live = place_ref[0], place_ref[1], place_ref[2]
    power_ref[...] = jnp.zeros_like(power_ref)
    grad_ref[...] = jnp.zeros_like(grad_ref)

    def stacked(flat):
        return jnp.concatenate([flat[:, :width], flat[:, width:]], axis=0)

    def forward(mode, _):
        for part in range(2):
            turned = pltpu.roll(probe_ref[mode, part], row, 0)
            rolled_ref[mode, part] = pltpu.roll(turned, col, 1)
        probe_re, probe_im = rolled_ref[mode, 0], rolled_ref[mode, 1]
        obj_re, obj_im = patch_ref[0], patch_ref[1]
        exit_wave = jnp.concatenate(
            [probe_re * obj_re - probe_im * obj_im, probe_re * obj_im + probe_im * obj_re], axis=1
        )
        wave = dot_left(cl_ref[...], stacked(dot_right(exit_wave, pr_ref[...])))
        wave_ref[mode] = wave
        power_ref[...] += wave[:width] * wave[:width] + wave[width:] * wave[width:]
        return 0

    def backward(mode, _):
        resid = power_ref[...]
        bent = jnp.concatenate([resid * wave_ref[mode, :width], resid * wave_ref[mode, width:]], axis=1)
        back = dot_left(pl_ref[...], stacked(dot_right(bent, cr_ref[...])))
        probe_re, probe_im = rolled_ref[mode, 0], rolled_ref[mode, 1]
        grad_ref[0] += probe_re * back[:width] + probe_im * back[width:]
        grad_ref[1] += probe_re * back[width:] - probe_im * back[:width]
        return 0

    lax.fori_loop(0, modes, forward, 0)
    power_ref[...] = jnp.where(live > 0, power_ref[...] - measured_ref[...], 0.0)
    lax.fori_loop(0, modes, backward, 0)


def slot_grad(place, patch, probe, measured):
    modes, width = probe.shape[0], probe.shape[-1]
    vmem = pl.BlockSpec(memory_space=pltpu.VMEM)
    work = 16 * modes * width**3 * 2 * 3
    return pl.pallas_call(
        slot_kernel,
        out_shape=jax.ShapeDtypeStruct(patch.shape, jnp.float32),
        in_specs=[pl.BlockSpec(memory_space=pltpu.SMEM)] + [vmem] * 7,
        out_specs=vmem,
        scratch_shapes=[
            pltpu.VMEM((modes, 2 * width, width), jnp.float32),
            pltpu.VMEM(probe.shape, jnp.float32),
            pltpu.VMEM((width, width), jnp.float32),
        ],
        compiler_params=pltpu.CompilerParams(vmem_limit_bytes=40 * 2**20),
        cost_estimate=pl.CostEstimate(flops=work, bytes_accessed=8 * 2**20, transcendentals=0),
        name="slot_grad",
    )(place, patch, probe, measured, *[jnp.asarray(t) for t in tables(width)])


def final_kernel(place_ref, base_ref, own_ref, other_ref, up_ref, up_other_ref, spill_ref, out_ref):
    width = own_ref.shape[-1]
    block = pl.program_id(0)
    shape = (width, width)
    rows = lax.broadcasted_iota(jnp.int32, shape, 0)
    cols = lax.broadcasted_iota(jnp.int32, shape, 1) + block * width
    masks = []
    for which in range(4):
        row, col = place_ref[2 * which], place_ref[2 * which + 1]
        inside = (cols >= col) & (cols < col + width)
        masks.append(inside & ((rows >= row) if which < 2 else (rows < row)))
    first = block == 0
    for part in range(2):
        total = jnp.where(first, spill_ref[part], 0.0)
        for mask, ref in zip(masks, (own_ref, other_ref, up_ref, up_other_ref)):
            total += jnp.where(mask, ref[part], 0.0)
        out_ref[part] = base_ref[part] - step_size * total


def final(place, base, own, other, up, up_other, spill):
    width = own.shape[-1]
    blocks = base.shape[2] // width
    whole = pl.BlockSpec((2, width, width), lambda k: (0, 0, 0))
    strip = pl.BlockSpec((2, width, width), lambda k: (0, 0, k))
    return pl.pallas_call(
        final_kernel,
        grid=(blocks,),
        out_shape=jax.ShapeDtypeStruct(base.shape, jnp.float32),
        in_specs=[pl.BlockSpec(memory_space=pltpu.SMEM), strip] + [whole] * 5,
        out_specs=strip,
        compiler_params=pltpu.CompilerParams(vmem_limit_bytes=40 * 2**20),
        name="final",
    )(place, base, own, other, up, up_other, spill)


def prior_base(obj, gram, top, bottom, left, right, first_row, first_col):
    tall = jnp.concatenate([top, obj, bottom], axis=1)
    window = jnp.concatenate([left, tall, right], axis=2)
    rows, cols = obj.shape[1], obj.shape[2]
    above, here, below = window[:, :rows], window[:, 1 : rows + 1], window[:, 2:]
    inner_row = jnp.logical_not(first_row & (jnp.arange(rows) == 0)).astype(jnp.float32)[None, :, None]
    inner_col = jnp.logical_not(first_col & (jnp.arange(cols) == 0)).astype(jnp.float32)[None, None, :]
    g = gram
    a = here[:, :, 1:-1]
    b = below[:, :, 1:-1]
    u = above[:, :, 1:-1]
    middle = g[0, 0] * a + g[0, 2] * b + inner_row * (g[2, 0] * u + g[2, 2] * a)
    middle += inner_col * (g[1, 1] * a + g[1, 3] * b + inner_row * (g[3, 1] * u + g[3, 3] * a))
    a, b, u = here[:, :, 2:], below[:, :, 2:], above[:, :, 2:]
    middle += g[0, 1] * a + g[0, 3] * b + inner_row * (g[2, 1] * u + g[2, 3] * a)
    a, b, u = here[:, :, :-2], below[:, :, :-2], above[:, :, :-2]
    middle += inner_col * (g[1, 0] * a + g[1, 2] * b + inner_row * (g[3, 0] * u + g[3, 2] * a))
    return obj - step_size * middle


def fold(tile, right, col):
    width = right.shape[2]
    ramp = jnp.arange(width, dtype=jnp.int32)[None, None, :]
    start = tile.shape[2]
    total = jnp.where(start + ramp < col + width, right, 0.0)
    for k in range(tile.shape[2] // width):
        place = k * width + ramp
        total = jnp.where((place >= col) & (place < col + width), tile[:, :, k * width : (k + 1) * width], total)
    return total


def local(tx, ty, obj, probe, intensity, offsets, counts, patch_filters):
    rows, cols = obj.shape[1], obj.shape[2]
    width = intensity.shape[-1]
    move = functools.partial(shift, tx=tx, ty=ty)
    here_tx, here_ty, mode = lax.axis_index("tx"), lax.axis_index("ty"), lax.axis_index("mode")

    tile_offsets = offsets[0, 0]
    up_offsets = move(tile_offsets, 1, 0)
    right = move(obj[:, :, :width], 0, -1)

    local_modes = probe.shape[0]
    half = local_modes // 2
    odd = lax.rem(here_tx, 2)
    mine = lax.dynamic_slice_in_dim(probe, odd * half, half, 0)
    fetched = lax.ppermute(mine, "mode", [(0, 1), (1, 0)])
    traded = lax.ppermute(fetched, "tx", [(i, i ^ 1) for i in range(tx)])
    chosen_probe = jnp.concatenate([probe, fetched, traded], axis=0)

    gram = jnp.dot(patch_filters.T, patch_filters, precision=highest)
    top = move(obj[:, rows - 1 :, :], 1, 0)
    bottom = move(obj[:, :1, :], -1, 0)
    edge_last = jnp.concatenate([top[:, :, -1:], obj[:, :, -1:], bottom[:, :, -1:]], axis=1)
    edge_first = jnp.concatenate([top[:, :, :1], obj[:, :, :1], bottom[:, :, :1]], axis=1)
    halo_left = move(edge_last, 0, 1)
    halo_right = move(edge_first, 0, -1)
    base = prior_base(obj, gram, top, bottom, halo_left, halo_right, here_tx == 0, here_ty == 0)

    my_place = lax.dynamic_index_in_dim(tile_offsets, mode, 0, False)
    my_up = lax.dynamic_index_in_dim(up_offsets, mode, 0, False)
    measured = lax.dynamic_index_in_dim(intensity[0, 0], mode, 0, False)
    below = move(fold(obj, right, my_up[1]), -1, 0)
    ramp = jnp.arange(width, dtype=jnp.int32)
    patch = jnp.where(ramp[None, :, None] >= my_place[0], fold(obj, right, my_place[1]), below)
    live = (mode < counts[0, 0]).astype(jnp.int32)
    place = jnp.stack([my_place[0] % width, my_place[1] % width, live])
    grad = slot_grad(place, patch, chosen_probe, measured)

    other = lax.ppermute(grad, "mode", [(0, 1), (1, 0)])
    up = move(grad, 1, 0)
    up_other = move(other, 1, 0)
    your_place = lax.dynamic_index_in_dim(tile_offsets, 1 - mode, 0, False)
    your_up = lax.dynamic_index_in_dim(up_offsets, 1 - mode, 0, False)

    row_ramp, col_ramp = ramp[None, :, None], ramp[None, None, :]

    def spilled(value, at, own):
        seen = col_ramp + cols < at[1] + width
        return jnp.where(seen & ((row_ramp >= at[0]) if own else (row_ramp < at[0])), value, 0.0)

    leaving = spilled(grad, my_place, True) + spilled(other, your_place, True)
    leaving += spilled(up, my_up, False) + spilled(up_other, your_up, False)
    spill = move(leaving, 0, 1)
    places = jnp.concatenate([my_place, your_place, my_up, your_up])
    return final(places, base, grad, other, up, up_other, spill)


def solution(mesh):
    placed = (
        P(None, "tx", "ty"),
        P("mode", None, None, None),
        P("tx", "ty", None, None, None),
        P("tx", "ty", None, None),
        P("tx", "ty"),
        P(),
    )
    return jax.shard_map(
        functools.partial(local, mesh.shape["tx"], mesh.shape["ty"]),
        mesh=mesh,
        in_specs=placed,
        out_specs=P(None, "tx", "ty"),
        check_vma=False,
    )
```

profile of v0, /device:TPU:16, one launch (start us, length us, event | category | flops | bytes accessed | tf_op | source)
XLA Modules:
  0.0 108.8 jit_solution(14586941439912611456)
XLA Ops:
  0.0 2.2 %collective-permute-start = (s32[2,2]{1,0:T(2,128)}, s32[2,2]{1,0:T(2,128)}, u32[]{:S(2)}, u32[]{:S(2)}) collective-permute-start(s32[2,2]{1,0:T(2,128)} %bitcast.42), channel_id=1, source_target_pairs={{0,4},{4,8},{8,12},{12,16},{16,20},{20,24},{24,28},{1,5},{5,9},{9,... | collective-permute-start | bytes 56 | tf_op jit(solution)/shard_map/ppermute | solution.py:28
  2.2 1.5 %fusion.21 = (f32[2,1,1024]{2,1,0:T(1,128)}, f32[2,1,1024]{2,1,0:T(1,128)}) fusion(f32[2,256,1024]{2,1,0:T(8,128)} %param.10), kind=kLoop, calls=%fused_computation.65 | loop fusion | bytes 32768 | tf_op jit(solution)/shard_map/slice | solution.py:210
  3.7 3.6 %collective-permute-start.1 = (f32[2,1,1024]{2,1,0:T(1,128)}, f32[2,1,1024]{2,1,0:T(1,128)S(1)}, u32[]{:S(2)}, u32[]{:S(2)}) collective-permute-start(f32[2,1,1024]{2,1,0:T(1,128)} %get-tuple-element.10), channel_id=1, source_target_pairs={{4,0},{8,4},{12,8},{16,12},{20,16},{24,20},{28,24},{5,1},{9,5},{13... | collective-permute-start | bytes 24584 | tf_op jit(solution)/shard_map/ppermute | solution.py:28
  7.3 1.9 %collective-permute-start.2 = (f32[2,1,1024]{2,1,0:T(1,128)}, f32[2,1,1024]{2,1,0:T(1,128)}, u32[]{:S(2)}, u32[]{:S(2)}) collective-permute-start(f32[2,1,1024]{2,1,0:T(1,128)} %get-tuple-element.9), channel_id=1, source_target_pairs={{0,4},{4,8},{8,12},{12,16},{16,20},{20,24},{24,28},{1,5},{5,9},{9,... | collective-permute-start | bytes 24584 | tf_op jit(solution)/shard_map/ppermute | solution.py:28
  9.3 1.9 %slice.211 = f32[2,256,256]{2,1,0:T(8,128)} slice(f32[2,256,1024]{2,1,0:T(8,128)} %param.10), slice={[0:2], [0:256], [0:256]} | slice | bytes 1048576 | tf_op jit(solution)/shard_map/slice | solution.py:187
  11.1 1.3 %collective-permute-start.5 = (f32[2,256,256]{2,1,0:T(8,128)}, f32[2,256,256]{2,1,0:T(8,128)S(1)}, u32[]{:S(2)}, u32[]{:S(2)}) collective-permute-start(f32[2,256,256]{2,1,0:T(8,128)} %slice.211), channel_id=1, source_target_pairs={{2,0},{3,1},{6,4},{7,5},{10,8},{11,9},{14,12},{15,13},{18,16},{19,... | collective-permute-start | bytes 1572872 | tf_op jit(solution)/shard_map/ppermute | solution.py:28
  12.4 1.9 %constant_dynamic-slice_fusion = f32[1,2,256,256]{3,2,1,0:T(8,128)} fusion(f32[2,2,256,256]{3,2,1,0:T(8,128)} %param.11, s32[]{:T(128)S(6)} %select_n.89), kind=kLoop, calls=%fused_computation.45 | loop fusion | bytes 1048580 | tf_op jit(solution)/shard_map/dynamic_slice | solution.py:204
  14.3 1.5 %collective-permute-start.7 = (f32[1,2,256,256]{3,2,1,0:T(8,128)}, f32[1,2,256,256]{3,2,1,0:T(8,128)}, u32[]{:S(2)}, u32[]{:S(2)}) collective-permute-start(f32[1,2,256,256]{3,2,1,0:T(8,128)} %constant_dynamic-slice_fusion), channel_id=1, source_target_pairs={{0,1},{1,0},{2,3},{3,2},{4,5},{5,4},{6,7},{7,6},{8,9},{9,8},{10,11... | collective-permute-start | bytes 1572872 | tf_op jit(solution)/shard_map/ppermute | solution.py:205
  24.4 1.2 %compare_and_fusion.5 = pred[256]{0:T(512)(128)(4,1)} fusion(s32[]{:T(128)S(6)} %add.208, s32[]{:T(128)} %bitcast.23), kind=kLoop, calls=%fused_computation.41 | loop fusion | flops 1024 | bytes 264 | tf_op jit(solution)/shard_map/and | solution.py:187
  38.8 1.5 %collective-permute-start.8 = (f32[1,2,256,256]{3,2,1,0:T(8,128)}, f32[1,2,256,256]{3,2,1,0:T(8,128)S(1)}, u32[]{:S(2)}, u32[]{:S(2)}) collective-permute-start(f32[1,2,256,256]{3,2,1,0:T(8,128)} %collective-permute-done.7), channel_id=1, source_target_pairs={{0,4},{4,0},{8,12},{12,8},{16,20},{20,16},{24,28},{28,24},{1,5},{5... | collective-permute-start | bytes 1572872 | tf_op jit(solution)/shard_map/ppermute | solution.py:206
  40.5 2.0 %collective-permute-start.6 = (f32[2,256,256]{2,1,0:T(8,128)S(1)}, f32[2,256,256]{2,1,0:T(8,128)S(1)}, u32[]{:S(2)}, u32[]{:S(2)}) collective-permute-start(f32[2,256,256]{2,1,0:T(8,128)S(1)} %select_select_fusion), channel_id=1, source_target_pairs={{4,0},{8,4},{12,8},{16,12},{20,16},{24,20},{28,24},{5,1},{9,5},{13... | collective-permute-start | bytes 1572872 | tf_op jit(solution)/shard_map/ppermute | solution.py:28
  43.4 1.4 %pad_maximum_fusion.3.probe_ref = f32[4,2,256,256]{3,2,1,0:T(8,128)S(1)} fusion(f32[1,2,256,256]{3,2,1,0:T(8,128)S(1)} %collective-permute-done.8, f32[1,2,256,256]{3,2,1,0:T(8,128)} %collective-permute-done.7, f32[2,2,256,256]{3,2,1,0:T(8,128)S(1)} %copy-done.6), kind=kLoop, calls=%fused_computation.21 | loop fusion | flops 1048576 | bytes 4194304 | tf_op jit(solution)/shard_map/concatenate | solution.py:207
  44.8 4.4 %collective-permute-done.6 = f32[2,256,256]{2,1,0:T(8,128)S(1)} collective-permute-done((f32[2,256,256]{2,1,0:T(8,128)S(1)}, f32[2,256,256]{2,1,0:T(8,128)S(1)}, u32[]{:S(2)}, u32[]{:S(2)}) %collective-permute-start.6) | collective-permute-done | bytes 524320 | tf_op jit(solution)/shard_map/ppermute | solution.py:28
  49.5 10.8 %slot_grad.1.own_ref = f32[2,256,256]{2,1,0:T(8,128)S(1)} custom-call(s32[3]{0:T(128)S(1)} %pad_add_fusion.1.place_ref, f32[2,256,256]{2,1,0:T(8,128)S(1)} %select_select_fusion.1.patch_ref, f32[4,2,256,256]{3,2,1,0:T(8,128)S(1)} %pad_maximum_fusion.3.probe_ref, f32[256,256]{1,0:T(8,128)S(1)} %dynamic-slice_bitcast_fusion.measured_ref, ...), custom_call_target="tpu_custom_call" | custom-call | flops 6442450944 | bytes 8388608 | tf_op jit(solution)/shard_map/slot_grad/pallas_call | solution.py:109
  61.9 1.3 %collective-permute-start.3 = (f32[2,258,1]{2,1,0:T(8,128)S(1)}, f32[2,258,1]{2,1,0:T(8,128)S(1)}, u32[]{:S(2)}, u32[]{:S(2)}) collective-permute-start(f32[2,258,1]{2,1,0:T(8,128)S(1)} %pad_maximum_fusion.4), channel_id=1, source_target_pairs={{2,0},{3,1},{6,4},{7,5},{10,8},{11,9},{14,12},{15,13},{18,16},{19,... | collective-permute-start | bytes 6200 | tf_op jit(solution)/shard_map/ppermute | solution.py:28
  63.2 4.6 %collective-permute-start.4 = (f32[2,258,1]{2,1,0:T(8,128)S(1)}, f32[2,258,1]{2,1,0:T(8,128)S(1)}, u32[]{:S(2)}, u32[]{:S(2)}) collective-permute-start(f32[2,258,1]{2,1,0:T(8,128)S(1)} %pad_maximum_fusion.5), channel_id=1, source_target_pairs={{0,2},{1,3},{4,6},{5,7},{8,10},{9,11},{12,14},{13,15},{16,18},{17,... | collective-permute-start | bytes 6200 | tf_op jit(solution)/shard_map/ppermute | solution.py:28
  67.8 3.0 %collective-permute-start.10 = (f32[2,256,256]{2,1,0:T(8,128)S(1)}, f32[2,256,256]{2,1,0:T(8,128)S(1)}, u32[]{:S(2)}, u32[]{:S(2)}) collective-permute-start(f32[2,256,256]{2,1,0:T(8,128)S(1)} %slot_grad.1.own_ref), channel_id=1, source_target_pairs={{0,4},{4,8},{8,12},{12,16},{16,20},{20,24},{24,28},{1,5},{5,9},{9,... | collective-permute-start | bytes 1572872 | tf_op jit(solution)/shard_map/ppermute | solution.py:28
  70.8 3.6 %collective-permute-done.9.other_ref = f32[2,256,256]{2,1,0:T(8,128)S(1)} collective-permute-done((f32[2,256,256]{2,1,0:T(8,128)S(1)}, f32[2,256,256]{2,1,0:T(8,128)S(1)}, u32[]{:S(2)}, u32[]{:S(2)}) %collective-permute-start.9) | collective-permute-done | bytes 524320 | tf_op jit(solution)/shard_map/ppermute | solution.py:228
  74.4 2.9 %collective-permute-start.11 = (f32[2,256,256]{2,1,0:T(8,128)S(1)}, f32[2,256,256]{2,1,0:T(8,128)S(1)}, u32[]{:S(2)}, u32[]{:S(2)}) collective-permute-start(f32[2,256,256]{2,1,0:T(8,128)S(1)} %collective-permute-done.9.other_ref), channel_id=1, source_target_pairs={{0,4},{4,8},{8,12},{12,16},{16,20},{20,24},{24,28},{1,5},{5,9},{9,... | collective-permute-start | bytes 1572872 | tf_op jit(solution)/shard_map/ppermute | solution.py:28
  77.4 1.7 %pad_maximum_fusion = (f32[2,258,1025]{2,1,0:T(8,128)S(1)}, f32[2,258,1025]{2,1,0:T(8,128)S(1)}) fusion(f32[2,258,1]{2,1,0:T(8,128)S(1)} %collective-permute-done.3, f32[2,1,1024]{2,1,0:T(1,128)S(1)} %collective-permute-done.1, f32[2,256,1024]{2,1,0:T(8,128)S(1)} %copy-done.5, f32[2,1,1024]{2,1,0:T(1,128)} %collective-permute-done.2, ...), kind=kLoop, calls=%fused_computation | loop fusion | flops 3173400 | bytes 6348864 | tf_op jit(solution)/shard_map/concatenate | solution.py:162
  79.2 5.7 %collective-permute-done.11.up_other_ref = f32[2,256,256]{2,1,0:T(8,128)S(1)} collective-permute-done((f32[2,256,256]{2,1,0:T(8,128)S(1)}, f32[2,256,256]{2,1,0:T(8,128)S(1)}, u32[]{:S(2)}, u32[]{:S(2)}) %collective-permute-start.11) | collective-permute-done | bytes 524320 | tf_op jit(solution)/shard_map/ppermute | solution.py:28
  85.1 4.3 %collective-permute-start.12 = (f32[2,256,256]{2,1,0:T(8,128)S(1)}, f32[2,256,256]{2,1,0:T(8,128)S(1)}, u32[]{:S(2)}, u32[]{:S(2)}) collective-permute-start(f32[2,256,256]{2,1,0:T(8,128)S(1)} %add_add_fusion), channel_id=1, source_target_pairs={{0,2},{1,3},{4,6},{5,7},{8,10},{9,11},{12,14},{13,15},{16,18},{17,... | collective-permute-start | bytes 1572872 | tf_op jit(solution)/shard_map/ppermute | solution.py:28
  89.4 16.0 %fusion.6.base_ref = f32[2,256,1024]{2,1,0:T(8,128)S(1)} fusion(f32[2,256,1024]{2,1,0:T(8,128)S(1)} %copy-done.5, f32[2,258,1025]{2,1,0:T(8,128)S(1)} %get-tuple-element.6, f32[2,258,1025]{2,1,0:T(8,128)S(1)} %get-tuple-element.5, f32[2,1,1024]{2,1,0:T(1,128)} %collective-permute-done.2, f32[2,1,1024]{2,1,0:T(1,128)S(1)} %collective-permute-done.1, ...), kind=kLoop, calls=%fused_computation.9 | loop fusion | flops 21495808 | bytes 16798784 | tf_op jit(solution)/shard_map/sub | solution.py:177
  105.5 3.3 %final.1 = f32[2,256,1024]{2,1,0:T(8,128)} custom-call(s32[8]{0:T(128)S(1)} %pad_add_fusion.place_ref, f32[2,256,1024]{2,1,0:T(8,128)S(1)} %fusion.6.base_ref, f32[2,256,256]{2,1,0:T(8,128)S(1)} %slot_grad.1.own_ref, f32[2,256,256]{2,1,0:T(8,128)S(1)} %collective-permute-done.9.other_ref, f32[2,256,256]{2,1,0:T(8,128)S(1)} %collective-permute-done.10.up_ref, ...), custom_call_target="tpu_custom_call" | custom-call | tf_op jit(solution)/shard_map/final/pallas_call | solution.py:149
  (103 shorter events, 17.6 us)
Async XLA Ops:
  0.0 29.9 %copy-start = (f32[1,1,2,256,256]{4,3,2,1,0:T(8,128)S(1)}, f32[1,1,2,256,256]{4,3,2,1,0:T(8,128)}, u32[]{:S(2)}) copy-start(f32[1,1,2,256,256]{4,3,2,1,0:T(8,128)} %param.12) | copy-start | bytes 1572868
  0.0 16.7 %copy-start.22 = (s32[1,1,2,2]{3,2,1,0:T(2,128)S(1)}, s32[1,1,2,2]{3,2,1,0:T(2,128)}, u32[]{:S(2)}) copy-start(s32[1,1,2,2]{3,2,1,0:T(2,128)} %param.13) | copy-start | bytes 52
  0.0 15.8 %copy-start.5 = (f32[2,256,1024]{2,1,0:T(8,128)S(1)}, f32[2,256,1024]{2,1,0:T(8,128)}, u32[]{:S(2)}) copy-start(f32[2,256,1024]{2,1,0:T(8,128)} %param.10) | copy-start | bytes 6291460
  0.0 27.8 %copy-start.9 = (f32[16,4]{0,1:T(4,128)S(1)}, f32[16,4]{0,1:T(4,128)}, u32[]{:S(2)}) copy-start(f32[16,4]{0,1:T(4,128)} %param.15) | copy-start | bytes 772
  0.0 32.3 %collective-permute-start = (s32[2,2]{1,0:T(2,128)}, s32[2,2]{1,0:T(2,128)}, u32[]{:S(2)}, u32[]{:S(2)}) collective-permute-start(s32[2,2]{1,0:T(2,128)} %bitcast.42), channel_id=1, source_target_pairs={{0,4},{4,8},{8,12},{12,16},{16,20},{20,24},{24,28},{1,5},{5,9},{9,... | collective-permute-start | bytes 56 | tf_op jit(solution)/shard_map/ppermute | solution.py:28
  3.7 57.3 %collective-permute-start.1 = (f32[2,1,1024]{2,1,0:T(1,128)}, f32[2,1,1024]{2,1,0:T(1,128)S(1)}, u32[]{:S(2)}, u32[]{:S(2)}) collective-permute-start(f32[2,1,1024]{2,1,0:T(1,128)} %get-tuple-element.10), channel_id=1, source_target_pairs={{4,0},{8,4},{12,8},{16,12},{20,16},{24,20},{28,24},{5,1},{9,5},{13... | collective-permute-start | bytes 24584 | tf_op jit(solution)/shard_map/ppermute | solution.py:28
  7.3 53.8 %collective-permute-start.2 = (f32[2,1,1024]{2,1,0:T(1,128)}, f32[2,1,1024]{2,1,0:T(1,128)}, u32[]{:S(2)}, u32[]{:S(2)}) collective-permute-start(f32[2,1,1024]{2,1,0:T(1,128)} %get-tuple-element.9), channel_id=1, source_target_pairs={{0,4},{4,8},{8,12},{12,16},{16,20},{20,24},{24,28},{1,5},{5,9},{9,... | collective-permute-start | bytes 24584 | tf_op jit(solution)/shard_map/ppermute | solution.py:28
  11.1 29.2 %collective-permute-start.5 = (f32[2,256,256]{2,1,0:T(8,128)}, f32[2,256,256]{2,1,0:T(8,128)S(1)}, u32[]{:S(2)}, u32[]{:S(2)}) collective-permute-start(f32[2,256,256]{2,1,0:T(8,128)} %slice.211), channel_id=1, source_target_pairs={{2,0},{3,1},{6,4},{7,5},{10,8},{11,9},{14,12},{15,13},{18,16},{19,... | collective-permute-start | bytes 1572872 | tf_op jit(solution)/shard_map/ppermute | solution.py:28
  14.3 24.5 %collective-permute-start.7 = (f32[1,2,256,256]{3,2,1,0:T(8,128)}, f32[1,2,256,256]{3,2,1,0:T(8,128)}, u32[]{:S(2)}, u32[]{:S(2)}) collective-permute-start(f32[1,2,256,256]{3,2,1,0:T(8,128)} %constant_dynamic-slice_fusion), channel_id=1, source_target_pairs={{0,1},{1,0},{2,3},{3,2},{4,5},{5,4},{6,7},{7,6},{8,9},{9,8},{10,11... | collective-permute-start | bytes 1572872 | tf_op jit(solution)/shard_map/ppermute | solution.py:205
  16.7 14.6 %copy-start.10 = (s32[1,1,1,2]{3,2,1,0:T(1,128)}, s32[1,1,1,2]{3,2,1,0:T(1,128)S(1)}, u32[]{:S(2)}) copy-start(s32[1,1,1,2]{3,2,1,0:T(1,128)S(1)} %get-tuple-element.31) | copy-start | bytes 28
  16.7 14.6 %copy-start.12 = (s32[1,1,1,2]{3,2,1,0:T(1,128)}, s32[1,1,1,2]{3,2,1,0:T(1,128)S(1)}, u32[]{:S(2)}) copy-start(s32[1,1,1,2]{3,2,1,0:T(1,128)S(1)} %get-tuple-element.32) | copy-start | bytes 28
  38.8 4.6 %collective-permute-start.8 = (f32[1,2,256,256]{3,2,1,0:T(8,128)}, f32[1,2,256,256]{3,2,1,0:T(8,128)S(1)}, u32[]{:S(2)}, u32[]{:S(2)}) collective-permute-start(f32[1,2,256,256]{3,2,1,0:T(8,128)} %collective-permute-done.7), channel_id=1, source_target_pairs={{0,4},{4,0},{8,12},{12,8},{16,20},{20,16},{24,28},{28,24},{1,5},{5... | collective-permute-start | bytes 1572872 | tf_op jit(solution)/shard_map/ppermute | solution.py:206
  40.5 8.7 %collective-permute-start.6 = (f32[2,256,256]{2,1,0:T(8,128)S(1)}, f32[2,256,256]{2,1,0:T(8,128)S(1)}, u32[]{:S(2)}, u32[]{:S(2)}) collective-permute-start(f32[2,256,256]{2,1,0:T(8,128)S(1)} %select_select_fusion), channel_id=1, source_target_pairs={{4,0},{8,4},{12,8},{16,12},{20,16},{24,20},{28,24},{5,1},{9,5},{13... | collective-permute-start | bytes 1572872 | tf_op jit(solution)/shard_map/ppermute | solution.py:28
  49.5 13.7 %copy-start.7 = (f32[2,256,1]{2,1,0:T(8,128)S(1)}, f32[2,256,1]{2,1,0:T(8,128)}, u32[]{:S(2)}) copy-start(f32[2,256,1]{2,1,0:T(8,128)} %get-tuple-element.8) | copy-start | bytes 6148
  49.5 27.8 %copy-start.11 = (s32[1,1,1,2]{3,2,1,0:T(1,128)S(1)}, s32[1,1,1,2]{3,2,1,0:T(1,128)}, u32[]{:S(2)}) copy-start(s32[1,1,1,2]{3,2,1,0:T(1,128)} %copy-done.10) | copy-start | bytes 28
  49.5 27.8 %copy-start.13 = (s32[1,1,1,2]{3,2,1,0:T(1,128)S(1)}, s32[1,1,1,2]{3,2,1,0:T(1,128)}, u32[]{:S(2)}) copy-start(s32[1,1,1,2]{3,2,1,0:T(1,128)} %copy-done.12) | copy-start | bytes 28
  49.5 27.8 %copy-start.15 = (s32[1,2]{1,0:T(1,128)S(1)}, s32[1,2]{1,0:T(1,128)}, u32[]{:S(2)}) copy-start(s32[1,2]{1,0:T(1,128)} %copy-done.14) | copy-start | bytes 28
  49.5 27.8 %copy-start.17 = (s32[1,2]{1,0:T(1,128)S(1)}, s32[1,2]{1,0:T(1,128)}, u32[]{:S(2)}) copy-start(s32[1,2]{1,0:T(1,128)} %copy-done.16) | copy-start | bytes 28
  60.4 14.0 %collective-permute-start.9 = (f32[2,256,256]{2,1,0:T(8,128)S(1)}, f32[2,256,256]{2,1,0:T(8,128)S(1)}, u32[]{:S(2)}, u32[]{:S(2)}) collective-permute-start(f32[2,256,256]{2,1,0:T(8,128)S(1)} %slot_grad.1.own_ref), channel_id=1, source_target_pairs={{0,1},{1,0},{2,3},{3,2},{4,5},{5,4},{6,7},{7,6},{8,9},{9,8},{10,11... | collective-permute-start | bytes 1572872 | tf_op jit(solution)/shard_map/ppermute | solution.py:228
  61.9 15.5 %collective-permute-start.3 = (f32[2,258,1]{2,1,0:T(8,128)S(1)}, f32[2,258,1]{2,1,0:T(8,128)S(1)}, u32[]{:S(2)}, u32[]{:S(2)}) collective-permute-start(f32[2,258,1]{2,1,0:T(8,128)S(1)} %pad_maximum_fusion.4), channel_id=1, source_target_pairs={{2,0},{3,1},{6,4},{7,5},{10,8},{11,9},{14,12},{15,13},{18,16},{19,... | collective-permute-start | bytes 6200 | tf_op jit(solution)/shard_map/ppermute | solution.py:28
  63.2 14.2 %collective-permute-start.4 = (f32[2,258,1]{2,1,0:T(8,128)S(1)}, f32[2,258,1]{2,1,0:T(8,128)S(1)}, u32[]{:S(2)}, u32[]{:S(2)}) collective-permute-start(f32[2,258,1]{2,1,0:T(8,128)S(1)} %pad_maximum_fusion.5), channel_id=1, source_target_pairs={{0,2},{1,3},{4,6},{5,7},{8,10},{9,11},{12,14},{13,15},{16,18},{17,... | collective-permute-start | bytes 6200 | tf_op jit(solution)/shard_map/ppermute | solution.py:28
  67.8 11.3 %collective-permute-start.10 = (f32[2,256,256]{2,1,0:T(8,128)S(1)}, f32[2,256,256]{2,1,0:T(8,128)S(1)}, u32[]{:S(2)}, u32[]{:S(2)}) collective-permute-start(f32[2,256,256]{2,1,0:T(8,128)S(1)} %slot_grad.1.own_ref), channel_id=1, source_target_pairs={{0,4},{4,8},{8,12},{12,16},{16,20},{20,24},{24,28},{1,5},{5,9},{9,... | collective-permute-start | bytes 1572872 | tf_op jit(solution)/shard_map/ppermute | solution.py:28
  74.4 10.5 %collective-permute-start.11 = (f32[2,256,256]{2,1,0:T(8,128)S(1)}, f32[2,256,256]{2,1,0:T(8,128)S(1)}, u32[]{:S(2)}, u32[]{:S(2)}) collective-permute-start(f32[2,256,256]{2,1,0:T(8,128)S(1)} %collective-permute-done.9.other_ref), channel_id=1, source_target_pairs={{0,4},{4,8},{8,12},{12,16},{16,20},{20,24},{24,28},{1,5},{5,9},{9,... | collective-permute-start | bytes 1572872 | tf_op jit(solution)/shard_map/ppermute | solution.py:28
  85.1 20.4 %collective-permute-start.12 = (f32[2,256,256]{2,1,0:T(8,128)S(1)}, f32[2,256,256]{2,1,0:T(8,128)S(1)}, u32[]{:S(2)}, u32[]{:S(2)}) collective-permute-start(f32[2,256,256]{2,1,0:T(8,128)S(1)} %add_add_fusion), channel_id=1, source_target_pairs={{0,2},{1,3},{4,6},{5,7},{8,10},{9,11},{12,14},{13,15},{16,18},{17,... | collective-permute-start | bytes 1572872 | tf_op jit(solution)/shard_map/ppermute | solution.py:28
  (16 other events, 99.5 us)
where the time goes:
time: 110 us; the launch traced here: 109 us
  other arithmetic  32 us (29%)
  starting transfers between devices  30.6 us (28%)
  Pallas kernels  14.2 us (13%)
  waiting for transfers between devices  13.7 us (12%)
  local copies, waits for them, and re-layouts  10.4 us (9%)
  between operations  7.82 us (7%)
    ppermute x10, starting transfers between devices, shift(): return lax.ppermute(value, axis, pairs)  27.1 us
    sub x1, other arithmetic, prior_base(): return obj - step_size * middle  16 us
    pallas_call x1, Pallas kernels, slot_grad(): pl.pallas_call(slot_kernel, out_shape=jax.ShapeDtypeStruct(patch.shape, j...  10.8 us
    ppermute x10, waiting for transfers between devices, shift(): return lax.ppermute(value, axis, pairs)  10.1 us
    and x8, other arithmetic, fold(): (place >= col) & (place < col + width)  7.13 us
    ppermute x1, waiting for transfers between devices, local(): other = lax.ppermute(grad, 'mode', [(0, 1), (1, 0)])  3.59 us
    pallas_call x1, Pallas kernels, final(): pl.pallas_call(final_kernel, grid=(blocks,), out_shape=jax.ShapeDtypeStru...  3.32 us
  transfers between devices with their start and end apart: 13, of which 3 were waited for; matrix products, arithmetic and copies ran while one was open for 38% of the time, Pallas kernels for 10%

commit v1 on v0

v1 whole, which is shorter than its diff:
```python
import functools
import math

import jax
import jax.numpy as jnp
import ml_dtypes
import numpy as np
from jax import lax
from jax.experimental import pallas as pl
from jax.experimental.pallas import tpu as pltpu
from jax.sharding import PartitionSpec as P

step_size = 0.25


def split(value):
    top = value.astype(np.float32).astype(ml_dtypes.bfloat16)
    rest = (value - top.astype(np.float64)).astype(ml_dtypes.bfloat16)
    return top, rest


def tables(length):
    ramp = np.arange(length)
    angle = (ramp[:, None] * ramp[None, :] % length) * (2.0 * math.pi / length)
    c = np.cos(angle) / math.sqrt(length)
    s = -np.sin(angle) / math.sqrt(length)
    plain = np.block([[c, s], [-s, c]])
    conj = np.block([[c, -s], [s, c]])
    out = []
    for table in (plain, conj):
        top, rest = split(table)
        out.append(np.concatenate([top, top, rest], axis=0))
        out.append(np.concatenate([top, top, rest], axis=1))
    return out


def halves(value):
    top = value.astype(jnp.bfloat16)
    rest = (value - top.astype(jnp.float32)).astype(jnp.bfloat16)
    return top, rest


def dot_right(value, table):
    top, rest = halves(value)
    return jnp.dot(jnp.concatenate([top, rest, top], axis=1), table, preferred_element_type=jnp.float32)


def dot_left(table, value):
    top, rest = halves(value)
    return jnp.dot(table, jnp.concatenate([top, rest, top], axis=0), preferred_element_type=jnp.float32)


MESH = pl.DeviceIdType.MESH
COPIES = 22


def step_kernel(
    tx, ty,
    offsets_ref, counts_ref, filters_ref, obj_hbm, probe_ref, intensity_hbm, pr_hbm, pl_hbm, cr_hbm, cl_hbm,
    out_ref,
    tall_ref, left_ref, right_ref, send_place, up_place, fetched_ref, traded_ref, turned_ref, fold_ref, up_fold_ref,
    below_ref, wave_ref, power_ref, measured_ref, grad_ref, other_ref, up_ref, up_other_ref, leave_ref, spill_ref,
    pr_ref, pl_ref, cr_ref, cl_ref, send_sem, recv_sem, local_sem,
):
    a, b, m = lax.axis_index("tx"), lax.axis_index("ty"), lax.axis_index("mode")
    rows, cols = obj_hbm.shape[1], obj_hbm.shape[2]
    width = power_ref.shape[-1]
    local_modes = probe_ref.shape[0]
    half = local_modes // 2
    modes = 2 * local_modes
    up = (lax.rem(a + tx - 1, tx), b, m)
    down = (lax.rem(a + 1, tx), b, m)
    left = (a, lax.rem(b + ty - 1, ty), m)
    right = (a, lax.rem(b + 1, ty), m)
    partner = (a, b, 1 - m)
    odd = lax.rem(a, 2)
    pair = (a + 1 - 2 * odd, b, m)

    def send(which, src, dst, target):
        copy = pltpu.make_async_remote_copy(
            src_ref=src, dst_ref=dst, send_sem=send_sem.at[which], recv_sem=recv_sem.at[which],
            device_id=target, device_id_type=MESH,
        )
        copy.start()
        return copy

    middle = pl.ds(8, rows)
    fetches = [
        pltpu.make_async_copy(src, dst, local_sem.at[k])
        for k, (src, dst) in enumerate((
            (obj_hbm, tall_ref.at[:, middle, :]),
            (intensity_hbm.at[0, 0, m], measured_ref),
            (pr_hbm, pr_ref), (cl_hbm, cl_ref), (cr_hbm, cr_ref), (pl_hbm, pl_ref),
        ))
    ]
    for fetch in fetches:
        fetch.start()

    row, col = offsets_ref[0, 0, m, 0], offsets_ref[0, 0, m, 1]
    your_row, your_col = offsets_ref[0, 0, 1 - m, 0], offsets_ref[0, 0, 1 - m, 1]
    for k, value in enumerate((row, col, your_row, your_col)):
        send_place[8 * k : 8 * k + 8] = jnp.full((8, width), value, jnp.int32)

    barrier = pltpu.get_barrier_semaphore()
    for target in (up, down, left, right, partner):
        pl.semaphore_signal(barrier, inc=1, device_id=target, device_id_type=MESH)
    pl.semaphore_wait(barrier, 5)

    copies = {}
    copies[0] = send(0, send_place, up_place, down)
    for part in range(2):
        copies[1 + part] = send(
            1 + part, obj_hbm.at[part, :, pl.ds(0, width)], right_ref.at[part, middle, :], left
        )
    copies[3] = send(3, probe_ref.at[pl.ds(odd * half, half)], fetched_ref, partner)
    copies[5] = send(5, obj_hbm.at[:, pl.ds(rows - 8, 8), :], tall_ref.at[:, pl.ds(0, 8), :], down)
    copies[6] = send(6, obj_hbm.at[:, pl.ds(0, 8), :], tall_ref.at[:, pl.ds(rows + 8, 8), :], up)
    copies[7] = send(7, obj_hbm.at[:, :, pl.ds(cols - 128, 128)], left_ref.at[:, middle, :], right)

    row_turn, col_turn = lax.rem(row, width), lax.rem(col, width)

    def turn(source, first, count):
        def one(mode, _):
            for part in range(2):
                turned = pltpu.roll(source[mode, part], row_turn, 0)
                turned_ref[first + mode, part] = pltpu.roll(turned, col_turn, 1)
            return 0

        lax.fori_loop(0, count, one, 0)

    shape = (width, width)
    row_ramp = lax.broadcasted_iota(jnp.int32, shape, 0)
    col_ramp = lax.broadcasted_iota(jnp.int32, shape, 1)

    def fold(part, at):
        total = jnp.where((col_ramp + cols < at + width) & (b < ty - 1), right_ref[part, middle, :], 0.0)
        for k in range(cols // width):
            place = col_ramp + k * width
            seen = (place >= at) & (place < at + width)
            total = jnp.where(seen, tall_ref[part, middle, k * width : (k + 1) * width], total)
        return total

    turn(probe_ref, 0, local_modes)
    fetches[0].wait()
    copies[0].wait_recv()
    copies[5].wait_recv()
    copies[6].wait_recv()
    top, bottom = pl.ds(0, 8), pl.ds(rows + 8, 8)
    copies[8] = send(8, tall_ref.at[:, top, pl.ds(cols - 128, 128)], left_ref.at[:, top, :], right)
    copies[9] = send(9, tall_ref.at[:, bottom, pl.ds(cols - 128, 128)], left_ref.at[:, bottom, :], right)
    up_row, up_col = up_place[0:1], up_place[8:9]
    up_your_row, up_your_col = up_place[16:17], up_place[24:25]
    for part in range(2):
        copies[1 + part].wait_recv()
        up_fold_ref[part] = fold(part, up_col)
        copies[12 + part] = send(12 + part, up_fold_ref.at[part], below_ref.at[part], up)
        fold_ref[part] = fold(part, col)
        if part == 0:
            copies[3].wait_recv()
            copies[4] = send(4, fetched_ref, traded_ref, pair)
            turn(fetched_ref, local_modes, half)
    copies[10] = send(10, tall_ref.at[:, top, pl.ds(0, 128)], right_ref.at[:, top, pl.ds(0, 128)], left)
    copies[11] = send(11, tall_ref.at[:, bottom, pl.ds(0, 128)], right_ref.at[:, bottom, pl.ds(0, 128)], left)
    copies[4].wait_recv()
    turn(traded_ref, local_modes + half, half)
    for fetch in fetches[1:]:
        fetch.wait()
    for part in range(2):
        copies[12 + part].wait_recv()
        below = jnp.where(a < tx - 1, below_ref[part], 0.0)
        fold_ref[part] = jnp.where(row_ramp >= row, fold_ref[part], below)

    power_ref[...] = jnp.zeros_like(power_ref)
    grad_ref[...] = jnp.zeros_like(grad_ref)

    def stacked(flat):
        return jnp.concatenate([flat[:, :width], flat[:, width:]], axis=0)

    def forward(mode, _):
        probe_re, probe_im = turned_ref[mode, 0], turned_ref[mode, 1]
        obj_re, obj_im = fold_ref[0], fold_ref[1]
        exit_wave = jnp.concatenate(
            [probe_re * obj_re - probe_im * obj_im, probe_re * obj_im + probe_im * obj_re], axis=1
        )
        wave = dot_left(cl_ref[...], stacked(dot_right(exit_wave, pr_ref[...])))
        wave_ref[mode] = wave
        power_ref[...] += wave[:width] * wave[:width] + wave[width:] * wave[width:]
        return 0

    def backward(mode, _):
        resid = power_ref[...]
        bent = jnp.concatenate([resid * wave_ref[mode, :width], resid * wave_ref[mode, width:]], axis=1)
        back = dot_left(pl_ref[...], stacked(dot_right(bent, cr_ref[...])))
        probe_re, probe_im = turned_ref[mode, 0], turned_ref[mode, 1]
        grad_ref[0] += probe_re * back[:width] + probe_im * back[width:]
        grad_ref[1] += probe_re * back[width:] - probe_im * back[:width]
        return 0

    lax.fori_loop(0, modes, forward, 0)
    power_ref[...] = jnp.where(m < counts_ref[0, 0], power_ref[...] - measured_ref[...], 0.0)
    lax.fori_loop(0, modes, backward, 0)

    for part in range(2):
        copies[14 + part] = send(14 + part, grad_ref.at[part], other_ref.at[part], partner)
        copies[16 + part] = send(16 + part, grad_ref.at[part], up_ref.at[part], down)

    gram = {}
    for i in range(4):
        for j in range(i, 4):
            total = filters_ref[0, i] * filters_ref[0, j]
            for f in range(1, filters_ref.shape[0]):
                total += filters_ref[f, i] * filters_ref[f, j]
            gram[i, j] = gram[j, i] = total
    for which in (7, 8, 9, 10, 11):
        copies[which].wait_recv()
    size = 64

    def prior(step, _):
        part = step // (rows // size)
        start = pl.multiple_of(lax.rem(step, rows // size) * size, size)

        def windows(ref, lanes):
            block = ref[part, pl.ds(start, size + 16), lanes]
            at = lax.broadcasted_iota(jnp.int32, (size, block.shape[1]), 0) + start
            low = jnp.where((at == rows - 1) & (a == tx - 1), 0.0, block[9 : size + 9])
            return block[7 : size + 7], block[8 : size + 8], low, jnp.logical_not((at == 0) & (a == 0))

        def side(sets, one, two, three, four):
            high, here, low, inner = sets
            return gram[one] * here + gram[two] * low + jnp.where(inner, gram[three] * high + gram[four] * here, 0.0)

        mid = windows(tall_ref, slice(None))
        lft = windows(left_ref, slice(None))
        rgt = windows(right_ref, slice(0, 128))
        inner_col = jnp.logical_not(
            (lax.broadcasted_iota(jnp.int32, (size, cols), 1) == 0) & (b == 0)
        )
        total = side(mid, (0, 0), (0, 2), (2, 0), (2, 2))
        ahead = side(mid, (0, 1), (0, 3), (2, 1), (2, 3))
        ahead_right = jnp.where(b < ty - 1, side(rgt, (0, 1), (0, 3), (2, 1), (2, 3)), 0.0)
        ahead = pltpu.roll(jnp.concatenate([ahead, ahead_right], axis=1), cols + 127, 1)[:, :cols]
        back = side(mid, (1, 0), (1, 2), (3, 0), (3, 2))
        back_left = side(lft, (1, 0), (1, 2), (3, 0), (3, 2))
        back = pltpu.roll(jnp.concatenate([back_left, back], axis=1), 1, 1)[:, 128:]
        back += side(mid, (1, 1), (1, 3), (3, 1), (3, 3))
        total += ahead + jnp.where(inner_col, back, 0.0)
        out_ref[part, pl.ds(start, size), :] = mid[1] - step_size * total
        return 0

    lax.fori_loop(0, 2 * (rows // size), prior, 0)

    def settle(part, values):
        for k in range(cols // width):
            place = col_ramp + k * width
            total = None
            for value, at_row, at_col, own in values:
                mask = (place >= at_col) & (place < at_col + width)
                mask &= (row_ramp >= at_row) if own else ((row_ramp < at_row) & (a > 0))
                piece = jnp.where(mask, value, 0.0)
                total = piece if total is None else total + piece
            here = slice(k * width, (k + 1) * width)
            out_ref[part, :, here] = out_ref[part, :, here] - step_size * total

    def spilled(value, at_row, at_col, own):
        mask = col_ramp + cols < at_col + width
        mask &= (row_ramp >= at_row) if own else ((row_ramp < at_row) & (a > 0))
        return jnp.where(mask, value, 0.0)

    for part in range(2):
        copies[14 + part].wait_recv()
        copies[18 + part] = send(18 + part, other_ref.at[part], up_other_ref.at[part], down)
        copies[16 + part].wait_recv()
        pieces = [
            (grad_ref[part], row, col, True),
            (other_ref[part], your_row, your_col, True),
            (up_ref[part], up_row, up_col, False),
        ]
        leave_ref[part] = spilled(*pieces[0]) + spilled(*pieces[1]) + spilled(*pieces[2])
        settle(part, pieces)
    for part in range(2):
        copies[18 + part].wait_recv()
        piece = (up_other_ref[part], up_your_row, up_your_col, False)
        leave_ref[part] = leave_ref[part] + spilled(*piece)
        copies[20 + part] = send(20 + part, leave_ref.at[part], spill_ref.at[part], right)
    for part in range(2):
        settle(part, [(up_other_ref[part], up_your_row, up_your_col, False)])
    for part in range(2):
        copies[20 + part].wait_recv()
        out_ref[part, :, :width] = out_ref[part, :, :width] - step_size * jnp.where(b > 0, spill_ref[part], 0.0)
    for which in range(COPIES):
        copies[which].wait_send()


def local(tx, ty, obj, probe, intensity, offsets, counts, patch_filters):
    rows, cols = obj.shape[1], obj.shape[2]
    width = intensity.shape[-1]
    local_modes = probe.shape[0]
    half = local_modes // 2
    modes = 2 * local_modes
    f32 = jnp.float32
    plane = (2, width, width)
    vmem = pl.BlockSpec(memory_space=pltpu.VMEM)
    smem = pl.BlockSpec(memory_space=pltpu.SMEM)
    hbm = pl.BlockSpec(memory_space=pl.ANY)
    consts = [jnp.asarray(t) for t in tables(width)]
    return pl.pallas_call(
        functools.partial(step_kernel, tx, ty),
        out_shape=jax.ShapeDtypeStruct(obj.shape, f32),
        in_specs=[smem, smem, smem, hbm, vmem, hbm] + [hbm] * 4,
        out_specs=vmem,
        scratch_shapes=[
            pltpu.VMEM((2, rows + 16, cols), f32),
            pltpu.VMEM((2, rows + 16, 128), f32),
            pltpu.VMEM((2, rows + 16, width), f32),
            pltpu.VMEM((32, width), jnp.int32),
            pltpu.VMEM((32, width), jnp.int32),
            pltpu.VMEM((half, 2, width, width), f32),
            pltpu.VMEM((half, 2, width, width), f32),
            pltpu.VMEM((modes, 2, width, width), f32),
            pltpu.VMEM(plane, f32),
            pltpu.VMEM(plane, f32),
            pltpu.VMEM(plane, f32),
            pltpu.VMEM((modes, 2 * width, width), f32),
            pltpu.VMEM((width, width), f32),
            pltpu.VMEM((width, width), f32),
        ]
        + [pltpu.VMEM(plane, f32)] * 6
        + [pltpu.VMEM(t.shape, t.dtype) for t in consts]
        + [
            pltpu.SemaphoreType.DMA((COPIES,)),
            pltpu.SemaphoreType.DMA((COPIES,)),
            pltpu.SemaphoreType.DMA((6,)),
        ],
        compiler_params=pltpu.CompilerParams(
            collective_id=0, has_side_effects=True, vmem_limit_bytes=56 * 2**20
        ),
        cost_estimate=pl.CostEstimate(
            flops=16 * modes * width**3 * 6, bytes_accessed=12 * 2**20, transcendentals=0
        ),
        name="guidance_step",
    )(offsets, counts, patch_filters, obj, probe, intensity, *consts)


def solution(mesh):
    placed = (
        P(None, "tx", "ty"),
        P("mode", None, None, None),
        P("tx", "ty", None, None, None),
        P("tx", "ty", None, None),
        P("tx", "ty"),
        P(),
    )
    return jax.shard_map(
        functools.partial(local, mesh.shape["tx"], mesh.shape["ty"]),
        mesh=mesh,
        in_specs=placed,
        out_specs=P(None, "tx", "ty"),
        check_vma=False,
    )
```

time: 110 us -> 64.7 us (0.59)
  the two profiles are of different devices: /device:TPU:16 before, /device:TPU:0 now
where the time goes in v1:
time: 64.7 us; the launch traced here: 64.5 us
  Pallas kernels  59.3 us (92%)
  local copies, waits for them, and re-layouts  4.52 us (7%)
  between operations  0.66 us (1%)
    pallas_call x1, Pallas kernels, local(): pl.pallas_call(functools.partial(step_kernel, tx, ty), out_shape=jax.Shap...  59.3 us
    unnamed x2, local copies, waits for them, and re-layouts  4.52 us

profile of v1, /device:TPU:0, one launch (start us, length us, event | category | flops | bytes accessed | tf_op | source)
XLA Modules:
  0.0 64.5 jit_solution(17694684798794188775)
XLA Ops:
  0.7 1.4 %copy.11.filters_ref = f32[16,4]{1,0:T(8,128)} copy(f32[16,4]{0,1:T(4,128)} %param.15) | data formatting | bytes 512 | tf_op args[5]
  2.0 59.3 %guidance_step.1 = f32[2,256,1024]{2,1,0:T(8,128)} custom-call(s32[1,1,2,2]{3,2,1,0:T(2,128)} %offsets_ref.1, s32[1,1]{1,0:T(1,128)S(6)} %copy.13.counts_ref, f32[16,4]{1,0:T(8,128)} %copy.11.filters_ref, f32[2,256,1024]{2,1,0:T(8,128)} %obj_hbm.1, f32[2,2,256,256]{3,2,1,0:T(8,128)} %probe_ref.1, f32[1,1,2,256,256]{4,3,2,1,0:T(8,128)} %intensity_hbm.1, ...), custom_call_target="tpu_custom_call" | custom-call | flops 6442450944 | bytes 12582912 | tf_op jit(solution)/shard_map/guidance_step/pallas_call | solution.py:306
  61.3 3.2 %copy.14 = f32[2,256,1024]{2,1,0:T(8,128)} copy(f32[2,256,1024]{2,1,0:T(8,128)} %guidance_step.1) | data formatting | bytes 4194304

commit v2 on v1

v2 whole, which is shorter than its diff:
```python
import functools
import math

import jax
import jax.numpy as jnp
import ml_dtypes
import numpy as np
from jax import lax
from jax.experimental import pallas as pl
from jax.experimental.pallas import tpu as pltpu
from jax.sharding import PartitionSpec as P

step_size = 0.25


def split(value):
    top = value.astype(np.float32).astype(ml_dtypes.bfloat16)
    rest = (value - top.astype(np.float64)).astype(ml_dtypes.bfloat16)
    return top, rest


def tables(length):
    ramp = np.arange(length)
    angle = (ramp[:, None] * ramp[None, :] % length) * (2.0 * math.pi / length)
    c = np.cos(angle) / math.sqrt(length)
    s = -np.sin(angle) / math.sqrt(length)
    plain = np.block([[c, s], [-s, c]])
    conj = np.block([[c, -s], [s, c]])
    out = []
    for table in (plain, conj):
        top, rest = split(table)
        out.append(np.concatenate([top, top, rest], axis=0))
        out.append(np.concatenate([top, top, rest], axis=1))
    return out


def halves(value):
    top = value.astype(jnp.bfloat16)
    rest = (value - top.astype(jnp.float32)).astype(jnp.bfloat16)
    return top, rest


def dot_right(value, table):
    top, rest = halves(value)
    return jnp.dot(jnp.concatenate([top, rest, top], axis=1), table, preferred_element_type=jnp.float32)


def dot_left(table, value):
    top, rest = halves(value)
    return jnp.dot(table, jnp.concatenate([top, rest, top], axis=0), preferred_element_type=jnp.float32)


MESH = pl.DeviceIdType.MESH
SPLITS = 4
CHUNKS = 2 * SPLITS
COPIES = 10 + 6 * CHUNKS


def step_kernel(
    tx, ty,
    offsets_ref, counts_ref, filters_ref, obj_hbm, probe_hbm, intensity_hbm, pr_hbm, pl_hbm, cr_hbm, cl_hbm,
    out_ref,
    tall_ref, probe_ref, left_ref, right_ref, send_place, up_place, fetched_ref, traded_ref, turned_ref, fold_ref, up_fold_ref,
    below_ref, wave_ref, power_ref, measured_ref, grad_ref, other_ref, up_ref, up_other_ref, leave_ref, spill_ref,
    pr_ref, pl_ref, cr_ref, cl_ref, send_sem, recv_sem, local_sem,
):
    a, b, m = lax.axis_index("tx"), lax.axis_index("ty"), lax.axis_index("mode")
    rows, cols = obj_hbm.shape[1], obj_hbm.shape[2]
    width = power_ref.shape[-1]
    local_modes = probe_ref.shape[0]
    half = local_modes // 2
    modes = 2 * local_modes
    up = (lax.rem(a + tx - 1, tx), b, m)
    down = (lax.rem(a + 1, tx), b, m)
    left = (a, lax.rem(b + ty - 1, ty), m)
    right = (a, lax.rem(b + 1, ty), m)
    partner = (a, b, 1 - m)
    odd = lax.rem(a, 2)
    pair = (a + 1 - 2 * odd, b, m)

    has_up, has_down, has_left, has_right = a > 0, a < tx - 1, b > 0, b < ty - 1
    sent, awaited = [], {}

    def when(conditions, action):
        test = None
        for condition in conditions:
            test = condition if test is None else test & condition
        if test is None:
            action()
        else:
            pl.when(test)(action)

    def send(which, src, dst, target, go=(), come=()):
        copy = pltpu.make_async_remote_copy(
            src_ref=src, dst_ref=dst, send_sem=send_sem.at[which], recv_sem=recv_sem.at[which],
            device_id=target, device_id_type=MESH,
        )
        when(go, copy.start)
        sent.append((copy, go))
        awaited[which] = (copy, come)

    def arrive(which):
        copy, come = awaited[which]
        when(come, copy.wait_recv)

    block = rows // SPLITS

    def chunk(which):
        return which // SPLITS, which % SPLITS * block

    middle = pl.ds(8, rows)
    fetches = [
        pltpu.make_async_copy(src, dst, local_sem.at[k])
        for k, (src, dst) in enumerate((
            (probe_hbm, probe_ref),
            (obj_hbm, tall_ref.at[:, middle, :]),
            (intensity_hbm.at[0, 0, m], measured_ref),
            (pr_hbm, pr_ref), (cl_hbm, cl_ref), (cr_hbm, cr_ref), (pl_hbm, pl_ref),
        ))
    ]
    for fetch in fetches:
        fetch.start()

    row, col = offsets_ref[0, 0, m, 0], offsets_ref[0, 0, m, 1]
    your_row, your_col = offsets_ref[0, 0, 1 - m, 0], offsets_ref[0, 0, 1 - m, 1]
    for k, value in enumerate((row, col, your_row, your_col)):
        send_place[8 * k : 8 * k + 8] = jnp.full((8, width), value, jnp.int32)

    barrier = pltpu.get_barrier_semaphore()
    for target in (up, down, left, right, partner):
        pl.semaphore_signal(barrier, inc=1, device_id=target, device_id_type=MESH)
    pl.semaphore_wait(barrier, 5)

    send(0, send_place, up_place, down, (has_down,), (has_up,))
    for c in range(CHUNKS):
        part, start = chunk(c)
        send(
            10 + c, obj_hbm.at[part, pl.ds(start, block), pl.ds(0, width)],
            right_ref.at[part, pl.ds(8 + start, block), :], left, (has_left,), (has_right,),
        )
    send(1, probe_hbm.at[pl.ds(odd * half, half)], fetched_ref, partner)
    top, bottom = pl.ds(0, 8), pl.ds(rows + 8, 8)
    send(3, obj_hbm.at[:, pl.ds(rows - 8, 8), :], tall_ref.at[:, top, :], down, (has_down,), (has_up,))
    send(4, obj_hbm.at[:, pl.ds(0, 8), :], tall_ref.at[:, bottom, :], up, (has_up,), (has_down,))
    send(5, obj_hbm.at[:, :, pl.ds(cols - 128, 128)], left_ref.at[:, middle, :], right, (has_right,), (has_left,))

    row_turn, col_turn = lax.rem(row, width), lax.rem(col, width)

    def turn(source, first, count):
        def one(mode, _):
            for part in range(2):
                turned = pltpu.roll(source[mode, part], row_turn, 0)
                turned_ref[first + mode, part] = pltpu.roll(turned, col_turn, 1)
            return 0

        lax.fori_loop(0, count, one, 0)

    block_shape = (block, width)
    col_ramp = lax.broadcasted_iota(jnp.int32, block_shape, 1)

    def row_ramp(start):
        return lax.broadcasted_iota(jnp.int32, block_shape, 0) + start

    def fold(part, start, at):
        lines = slice(8 + start, 8 + start + block)
        total = jnp.where((col_ramp + cols < at + width) & has_right, right_ref[part, lines, :], 0.0)
        for k in range(cols // width):
            place = col_ramp + k * width
            seen = (place >= at) & (place < at + width)
            total = jnp.where(seen, tall_ref[part, lines, k * width : (k + 1) * width], total)
        return total

    fetches[0].wait()
    turn(probe_ref, 0, local_modes)
    fetches[1].wait()
    arrive(0)
    arrive(3)
    arrive(4)
    low, high = pl.ds(0, 128), pl.ds(cols - 128, 128)
    send(6, tall_ref.at[:, top, high], left_ref.at[:, top, :], right, (has_right, has_up), (has_left, has_up))
    send(7, tall_ref.at[:, bottom, high], left_ref.at[:, bottom, :], right, (has_right, has_down), (has_left, has_down))
    up_row, up_col = up_place[0:1], up_place[8:9]
    up_your_row, up_your_col = up_place[16:17], up_place[24:25]
    for c in range(CHUNKS):
        part, start = chunk(c)
        lines = slice(start, start + block)
        arrive(10 + c)
        up_fold_ref[part, lines] = fold(part, start, up_col)
        send(
            10 + CHUNKS + c, up_fold_ref.at[part, pl.ds(start, block)], below_ref.at[part, pl.ds(start, block)],
            up, (has_up,), (has_down,),
        )
        fold_ref[part, lines] = fold(part, start, col)
    arrive(1)
    send(2, fetched_ref, traded_ref, pair)
    send(8, tall_ref.at[:, top, low], right_ref.at[:, top, low], left, (has_left, has_up), (has_right, has_up))
    send(9, tall_ref.at[:, bottom, low], right_ref.at[:, bottom, low], left, (has_left, has_down), (has_right, has_down))
    turn(fetched_ref, local_modes, half)
    arrive(2)
    turn(traded_ref, local_modes + half, half)
    for fetch in fetches[2:]:
        fetch.wait()
    for c in range(CHUNKS):
        part, start = chunk(c)
        lines = slice(start, start + block)
        arrive(10 + CHUNKS + c)
        below = jnp.where(has_down, below_ref[part, lines], 0.0)
        fold_ref[part, lines] = jnp.where(row_ramp(start) >= row, fold_ref[part, lines], below)

    power_ref[...] = jnp.zeros_like(power_ref)
    grad_ref[...] = jnp.zeros_like(grad_ref)

    def stacked(flat):
        return jnp.concatenate([flat[:, :width], flat[:, width:]], axis=0)

    def forward(mode, _):
        probe_re, probe_im = turned_ref[mode, 0], turned_ref[mode, 1]
        obj_re, obj_im = fold_ref[0], fold_ref[1]
        exit_wave = jnp.concatenate(
            [probe_re * obj_re - probe_im * obj_im, probe_re * obj_im + probe_im * obj_re], axis=1
        )
        wave = dot_left(cl_ref[...], stacked(dot_right(exit_wave, pr_ref[...])))
        wave_ref[mode] = wave
        power_ref[...] += wave[:width] * wave[:width] + wave[width:] * wave[width:]
        return 0

    def backward(mode, _):
        resid = power_ref[...]
        bent = jnp.concatenate([resid * wave_ref[mode, :width], resid * wave_ref[mode, width:]], axis=1)
        back = dot_left(pl_ref[...], stacked(dot_right(bent, cr_ref[...])))
        probe_re, probe_im = turned_ref[mode, 0], turned_ref[mode, 1]
        grad_ref[0] += probe_re * back[:width] + probe_im * back[width:]
        grad_ref[1] += probe_re * back[width:] - probe_im * back[:width]
        return 0

    lax.fori_loop(0, modes, forward, 0)
    power_ref[...] = jnp.where(m < counts_ref[0, 0], power_ref[...] - measured_ref[...], 0.0)
    lax.fori_loop(0, modes, backward, 0)

    other_at, up_at, up_other_at, spill_at = (10 + k * CHUNKS for k in range(2, 6))

    def piece_of(ref, which):
        part, start = chunk(which)
        return ref.at[part, pl.ds(start, block)]

    for c in range(CHUNKS):
        send(other_at + c, piece_of(grad_ref, c), piece_of(other_ref, c), partner)
        send(up_at + c, piece_of(grad_ref, c), piece_of(up_ref, c), down, (has_down,), (has_up,))

    gram = {}
    for i in range(4):
        for j in range(i, 4):
            total = filters_ref[i, 0] * filters_ref[j, 0]
            for f in range(1, filters_ref.shape[1]):
                total += filters_ref[i, f] * filters_ref[j, f]
            gram[i, j] = gram[j, i] = total
    for which in range(5, 10):
        arrive(which)
    size = block

    def prior(part, start):

        def windows(ref, lanes):
            block = ref[part, pl.ds(start, size + 16), lanes]
            at = lax.broadcasted_iota(jnp.int32, (size, block.shape[1]), 0) + start
            low = jnp.where((at == rows - 1) & jnp.logical_not(has_down), 0.0, block[9 : size + 9])
            return block[7 : size + 7], block[8 : size + 8], low, jnp.logical_not((at == 0) & (a == 0))

        def side(sets, one, two, three, four):
            high, here, low, inner = sets
            return gram[one] * here + gram[two] * low + jnp.where(inner, gram[three] * high + gram[four] * here, 0.0)

        mid = windows(tall_ref, slice(None))
        lft = windows(left_ref, slice(None))
        rgt = windows(right_ref, slice(0, 128))
        inner_col = jnp.logical_not(
            (lax.broadcasted_iota(jnp.int32, (size, cols), 1) == 0) & (b == 0)
        )
        total = side(mid, (0, 0), (0, 2), (2, 0), (2, 2))
        ahead = side(mid, (0, 1), (0, 3), (2, 1), (2, 3))
        ahead_right = jnp.where(has_right, side(rgt, (0, 1), (0, 3), (2, 1), (2, 3)), 0.0)
        ahead = pltpu.roll(jnp.concatenate([ahead, ahead_right], axis=1), cols + 127, 1)[:, :cols]
        back = side(mid, (1, 0), (1, 2), (3, 0), (3, 2))
        back_left = side(lft, (1, 0), (1, 2), (3, 0), (3, 2))
        back = pltpu.roll(jnp.concatenate([back_left, back], axis=1), 1, 1)[:, 128:]
        back += side(mid, (1, 1), (1, 3), (3, 1), (3, 3))
        total += ahead + jnp.where(inner_col, back, 0.0)
        out_ref[part, pl.ds(start, size), :] = mid[1] - step_size * total

    def settle(part, start, values):
        lines = slice(start, start + block)
        ramp = row_ramp(start)
        values = [
            (jnp.where((ramp >= at_row) if own else ((ramp < at_row) & has_up), value, 0.0), at_col)
            for value, at_row, at_col, own in values
        ]
        for k in range(cols // width):
            place = col_ramp + k * width
            total = None
            for value, at_col in values:
                piece = jnp.where((place >= at_col) & (place < at_col + width), value, 0.0)
                total = piece if total is None else total + piece
            here = slice(k * width, (k + 1) * width)
            out_ref[part, lines, here] = out_ref[part, lines, here] - step_size * total

    def spilled(start, value, at_row, at_col, own):
        ramp = row_ramp(start)
        mask = col_ramp + cols < at_col + width
        mask &= (ramp >= at_row) if own else ((ramp < at_row) & has_up)
        return jnp.where(mask, value, 0.0)

    lag = 2
    for step in range(CHUNKS + lag):
        if step < CHUNKS:
            part, start = chunk(step)
            arrive(other_at + step)
            send(
                up_other_at + step, piece_of(other_ref, step), piece_of(up_other_ref, step), down,
                (has_down,), (has_up,),
            )
        if step >= lag:
            late = step - lag
            part, start = chunk(late)
            lines = slice(start, start + block)
            arrive(up_other_at + late)
            last = (up_other_ref[part, lines], up_your_row, up_your_col, False)
            leave_ref[part, lines] = leave_ref[part, lines] + spilled(start, *last)
            send(
                spill_at + late, piece_of(leave_ref, late), piece_of(spill_ref, late), right,
                (has_right,), (has_left,),
            )
            settle(part, start, [last])
        if step < CHUNKS:
            part, start = chunk(step)
            lines = slice(start, start + block)
            arrive(up_at + step)
            pieces = [
                (grad_ref[part, lines], row, col, True),
                (other_ref[part, lines], your_row, your_col, True),
                (up_ref[part, lines], up_row, up_col, False),
            ]
            leave_ref[part, lines] = (
                spilled(start, *pieces[0]) + spilled(start, *pieces[1]) + spilled(start, *pieces[2])
            )
            prior(part, start)
            settle(part, start, pieces)
    for c in range(CHUNKS):
        part, start = chunk(c)
        lines = slice(start, start + block)
        arrive(spill_at + c)
        spill = jnp.where(has_left, spill_ref[part, lines], 0.0)
        out_ref[part, lines, :width] = out_ref[part, lines, :width] - step_size * spill
    for copy, go in sent:
        when(go, copy.wait_send)


def local(tx, ty, obj, probe, intensity, offsets, counts, patch_filters):
    rows, cols = obj.shape[1], obj.shape[2]
    width = intensity.shape[-1]
    local_modes = probe.shape[0]
    half = local_modes // 2
    modes = 2 * local_modes
    f32 = jnp.float32
    plane = (2, width, width)
    vmem = pl.BlockSpec(memory_space=pltpu.VMEM)
    smem = pl.BlockSpec(memory_space=pltpu.SMEM)
    hbm = pl.BlockSpec(memory_space=pltpu.HBM)
    consts = [jnp.asarray(t) for t in tables(width)]
    return pl.pallas_call(
        functools.partial(step_kernel, tx, ty),
        out_shape=jax.ShapeDtypeStruct(obj.shape, f32),
        in_specs=[smem, smem, smem, hbm, hbm, hbm] + [hbm] * 4,
        out_specs=vmem,
        scratch_shapes=[
            pltpu.VMEM((2, rows + 16, cols), f32),
            pltpu.VMEM(probe.shape, f32),
            pltpu.VMEM((2, rows + 16, 128), f32),
            pltpu.VMEM((2, rows + 16, width), f32),
            pltpu.VMEM((32, width), jnp.int32),
            pltpu.VMEM((32, width), jnp.int32),
            pltpu.VMEM((half, 2, width, width), f32),
            pltpu.VMEM((half, 2, width, width), f32),
            pltpu.VMEM((modes, 2, width, width), f32),
            pltpu.VMEM(plane, f32),
            pltpu.VMEM(plane, f32),
            pltpu.VMEM(plane, f32),
            pltpu.VMEM((modes, 2 * width, width), f32),
            pltpu.VMEM((width, width), f32),
            pltpu.VMEM((width, width), f32),
        ]
        + [pltpu.VMEM(plane, f32)] * 6
        + [pltpu.VMEM(t.shape, t.dtype) for t in consts]
        + [
            pltpu.SemaphoreType.DMA((COPIES,)),
            pltpu.SemaphoreType.DMA((COPIES,)),
            pltpu.SemaphoreType.DMA((7,)),
        ],
        compiler_params=pltpu.CompilerParams(
            collective_id=0, has_side_effects=True, vmem_limit_bytes=40 * 2**20
        ),
        cost_estimate=pl.CostEstimate(
            flops=16 * modes * width**3 * 6, bytes_accessed=12 * 2**20, transcendentals=0
        ),
        name="guidance_step",
    )(offsets, counts, patch_filters.T, obj, probe, intensity, *consts)


def solution(mesh):
    placed = (
        P(None, "tx", "ty"),
        P("mode", None, None, None),
        P("tx", "ty", None, None, None),
        P("tx", "ty", None, None),
        P("tx", "ty"),
        P(),
    )
    return jax.shard_map(
        functools.partial(local, mesh.shape["tx"], mesh.shape["ty"]),
        mesh=mesh,
        in_specs=placed,
        out_specs=P(None, "tx", "ty"),
        check_vma=False,
    )
```

time: 64.7 us -> 63.4 us (0.980)
  the two profiles are of different devices: /device:TPU:0 before, /device:TPU:12 now
where the time goes in v2:
time: 63.4 us; the launch traced here: 63 us
  Pallas kernels  50.2 us (79%)
  local copies, waits for them, and re-layouts  12.2 us (19%)
  between operations  0.68 us (1%)
    pallas_call x1, Pallas kernels, local(): pl.pallas_call(functools.partial(step_kernel, tx, ty), out_shape=jax.Shap...  50.2 us
    unnamed x19, local copies, waits for them, and re-layouts  12.2 us

profile of v2, /device:TPU:12, one launch (start us, length us, event | category | flops | bytes accessed | tf_op | source)
XLA Modules:
  0.0 63.0 jit_solution(5115263406501872914)
XLA Ops:
  0.7 0.0 copy-start
  0.7 1.6 %copy-done = f32[2,256,1024]{2,1,0:T(8,128)S(1)} copy-done((f32[2,256,1024]{2,1,0:T(8,128)S(1)}, f32[2,256,1024]{2,1,0:T(8,128)}, u32[]{:S(2)}) %copy-start) | copy-done | bytes 2097176
  2.2 0.0 copy-start.1
  2.2 1.2 %copy-done.1 = f32[2,2,256,256]{3,2,1,0:T(8,128)S(1)} copy-done((f32[2,2,256,256]{3,2,1,0:T(8,128)S(1)}, f32[2,2,256,256]{3,2,1,0:T(8,128)}, u32[]{:S(2)}) %copy-start.1) | copy-done | bytes 1048600
  3.5 0.0 copy-start.2
  3.5 1.0 %copy-done.2 = f32[1,1,2,256,256]{4,3,2,1,0:T(8,128)S(1)} copy-done((f32[1,1,2,256,256]{4,3,2,1,0:T(8,128)S(1)}, f32[1,1,2,256,256]{4,3,2,1,0:T(8,128)}, u32[]{:S(2)}) %copy-start.2) | copy-done | bytes 524312
  4.5 0.0 copy-start.3
  4.5 0.7 %copy-done.3 = f32[16,4]{0,1:T(4,128)S(1)} copy-done((f32[16,4]{0,1:T(4,128)S(1)}, f32[16,4]{0,1:T(4,128)}, u32[]{:S(2)}) %copy-start.3) | copy-done | bytes 280
  5.2 0.0 copy-start.4
  5.2 0.7 %copy-done.4 = s32[1,1,2,2]{3,2,1,0:T(2,128)S(1)} copy-done((s32[1,1,2,2]{3,2,1,0:T(2,128)S(1)}, s32[1,1,2,2]{3,2,1,0:T(2,128)}, u32[]{:S(2)}) %copy-start.4) | copy-done | bytes 40
  5.9 0.0 copy-start.5
  5.9 1.4 %copy-done.5 = bf16[512,1536]{1,0:T(8,128)(2,1)S(1)} copy-done((bf16[512,1536]{1,0:T(8,128)(2,1)S(1)}, bf16[512,1536]{1,0:T(8,128)(2,1)}, u32[]{:S(2)}) %copy-start.5) | copy-done | bytes 1572888
  7.3 0.0 copy-start.6
  7.3 1.4 %copy-done.6 = bf16[1536,512]{1,0:T(8,128)(2,1)S(1)} copy-done((bf16[1536,512]{1,0:T(8,128)(2,1)S(1)}, bf16[1536,512]{1,0:T(8,128)(2,1)}, u32[]{:S(2)}) %copy-start.6) | copy-done | bytes 1572888
  8.7 0.0 copy-start.7
  8.7 1.4 %copy-done.7 = bf16[512,1536]{1,0:T(8,128)(2,1)S(1)} copy-done((bf16[512,1536]{1,0:T(8,128)(2,1)S(1)}, bf16[512,1536]{1,0:T(8,128)(2,1)}, u32[]{:S(2)}) %copy-start.7) | copy-done | bytes 1572888
  10.1 0.0 copy-start.8
  10.1 1.4 %copy-done.8 = bf16[1536,512]{1,0:T(8,128)(2,1)S(1)} copy-done((bf16[1536,512]{1,0:T(8,128)(2,1)S(1)}, bf16[1536,512]{1,0:T(8,128)(2,1)}, u32[]{:S(2)}) %copy-start.8) | copy-done | bytes 1572888
  11.5 50.2 %guidance_step.1 = f32[2,256,1024]{2,1,0:T(8,128)S(1)} custom-call(s32[1,1,2,2]{3,2,1,0:T(2,128)S(1)} %copy-done.4, s32[1,1]{1,0:T(1,128)S(6)} %copy.12.counts_ref, f32[4,16]{1,0:T(4,128)S(1)} %bitcast.1, f32[2,256,1024]{2,1,0:T(8,128)S(1)} %copy-done, f32[2,2,256,256]{3,2,1,0:T(8,128)S(1)} %copy-done.1, f32[1,1,2,256,256]{4,3,2,1,0:T(8,128)S(1)} %copy-done.2, ...), custom_call_target="tpu_custom_call" | custom-call | flops 6442450944 | bytes 12582912 | tf_op jit(solution)/shard_map/guidance_step/pallas_call | solution.py:369
  61.7 1.3 %copy.13 = f32[2,256,1024]{2,1,0:T(8,128)} copy(f32[2,256,1024]{2,1,0:T(8,128)S(1)} %guidance_step.1) | data formatting | bytes 4194304
Async XLA Ops:
  0.7 1.6 %copy-start = (f32[2,256,1024]{2,1,0:T(8,128)S(1)}, f32[2,256,1024]{2,1,0:T(8,128)}, u32[]{:S(2)}) copy-start(f32[2,256,1024]{2,1,0:T(8,128)} %obj_hbm.1) | copy-start | bytes 6291460
  2.2 1.2 %copy-start.1 = (f32[2,2,256,256]{3,2,1,0:T(8,128)S(1)}, f32[2,2,256,256]{3,2,1,0:T(8,128)}, u32[]{:S(2)}) copy-start(f32[2,2,256,256]{3,2,1,0:T(8,128)} %probe_hbm.1) | copy-start | bytes 3145732
  3.5 1.0 %copy-start.2 = (f32[1,1,2,256,256]{4,3,2,1,0:T(8,128)S(1)}, f32[1,1,2,256,256]{4,3,2,1,0:T(8,128)}, u32[]{:S(2)}) copy-start(f32[1,1,2,256,256]{4,3,2,1,0:T(8,128)} %intensity_hbm.1) | copy-start | bytes 1572868
  4.5 0.7 %copy-start.3 = (f32[16,4]{0,1:T(4,128)S(1)}, f32[16,4]{0,1:T(4,128)}, u32[]{:S(2)}) copy-start(f32[16,4]{0,1:T(4,128)} %param.15) | copy-start | bytes 772
  5.2 0.7 %copy-start.4 = (s32[1,1,2,2]{3,2,1,0:T(2,128)S(1)}, s32[1,1,2,2]{3,2,1,0:T(2,128)}, u32[]{:S(2)}) copy-start(s32[1,1,2,2]{3,2,1,0:T(2,128)} %offsets_ref.1) | copy-start | bytes 52
  5.9 1.4 %copy-start.5 = (bf16[512,1536]{1,0:T(8,128)(2,1)S(1)}, bf16[512,1536]{1,0:T(8,128)(2,1)}, u32[]{:S(2)}) copy-start(bf16[512,1536]{1,0:T(8,128)(2,1)} %constant.11.clone.cl_hbm) | copy-start | bytes 4718596
  7.3 1.4 %copy-start.6 = (bf16[1536,512]{1,0:T(8,128)(2,1)S(1)}, bf16[1536,512]{1,0:T(8,128)(2,1)}, u32[]{:S(2)}) copy-start(bf16[1536,512]{1,0:T(8,128)(2,1)} %constant.10.clone.cr_hbm) | copy-start | bytes 4718596
  8.7 1.4 %copy-start.7 = (bf16[512,1536]{1,0:T(8,128)(2,1)S(1)}, bf16[512,1536]{1,0:T(8,128)(2,1)}, u32[]{:S(2)}) copy-start(bf16[512,1536]{1,0:T(8,128)(2,1)} %constant.9.clone.pl_hbm) | copy-start | bytes 4718596
  10.1 1.4 %copy-start.8 = (bf16[1536,512]{1,0:T(8,128)(2,1)S(1)}, bf16[1536,512]{1,0:T(8,128)(2,1)}, u32[]{:S(2)}) copy-start(bf16[1536,512]{1,0:T(8,128)(2,1)} %constant.8.clone.pr_hbm) | copy-start | bytes 4718596

commit v3 on v2

--- a/solution.py
+++ b/solution.py
@@ -396,7 +396,7 @@
             pltpu.SemaphoreType.DMA((7,)),
         ],
         compiler_params=pltpu.CompilerParams(
-            collective_id=0, has_side_effects=True, vmem_limit_bytes=40 * 2**20
+            collective_id=0, has_side_effects=True, vmem_limit_bytes=57 * 2**20
         ),
         cost_estimate=pl.CostEstimate(
             flops=16 * modes * width**3 * 6, bytes_accessed=12 * 2**20, transcendentals=0

time: 63.4 us -> 55.2 us (0.87)
  local copies, waits for them, and re-layouts: 12.2 us -> 3.16 us
  Pallas kernels: 50.2 us -> 51.2 us
    unnamed x19 -> x1, local copies, waits for them, and re-layouts: 12.2 us -> 3.16 us
    pallas_call x1, Pallas kernels: 50.2 us -> 51.2 us  [local(): pl.pallas_call(functools.partial(step_kernel, tx, ty), out_shape=jax.Shap...]
where the time goes in v3:
time: 55.2 us; the launch traced here: 55.1 us
  Pallas kernels  51.2 us (93%)
  local copies, waits for them, and re-layouts  3.16 us (6%)
  between operations  0.66 us (1%)
    pallas_call x1, Pallas kernels, local(): pl.pallas_call(functools.partial(step_kernel, tx, ty), out_shape=jax.Shap...  51.2 us
    unnamed x1, local copies, waits for them, and re-layouts  3.16 us

profile of v3, /device:TPU:12, one launch (start us, length us, event | category | flops | bytes accessed | tf_op | source)
XLA Modules:
  0.0 55.1 jit_solution(16301110503816846593)
XLA Ops:
  0.7 51.2 %guidance_step.1 = f32[2,256,1024]{2,1,0:T(8,128)} custom-call(s32[1,1,2,2]{3,2,1,0:T(2,128)} %offsets_ref.1, s32[1,1]{1,0:T(1,128)S(6)} %copy.12.counts_ref, f32[4,16]{1,0:T(4,128)} %bitcast.1, f32[2,256,1024]{2,1,0:T(8,128)} %obj_hbm.1, f32[2,2,256,256]{3,2,1,0:T(8,128)} %probe_hbm.1, f32[1,1,2,256,256]{4,3,2,1,0:T(8,128)} %intensity_hbm.1, ...), custom_call_target="tpu_custom_call" | custom-call | flops 6442450944 | bytes 12582912 | tf_op jit(solution)/shard_map/guidance_step/pallas_call | solution.py:369
  51.9 3.2 %copy.13 = f32[2,256,1024]{2,1,0:T(8,128)} copy(f32[2,256,1024]{2,1,0:T(8,128)} %guidance_step.1) | data formatting | bytes 4194304
